TPU v7x, 32 devices: a whole 2x2x4 slice. The times are simulated.
32 devices in a mesh: frames: 2 (over x), slabs: 16 (over z, y, core).
Axes of the slice: x: 2, y: 2, z: 4, core: 2. Of those that a mesh axis runs over, the one named last changes fastest.
Arguments:
- movie: bfloat16 [16, 32768], P('frames', 'slabs'), may hold values from -48 to 48
- traces: bfloat16 [16, 256], P('frames', 'slabs'), may hold values from -6 to 6
- voxel_index: int32 [256, 2048], P('slabs'), may hold values from 0 to 4095, as said below
- footprint: float32 [256, 2048], P('slabs'), may hold values from 0 to 1
- block_order: int32 [2], replicated, may hold values from 0 to 1, each once
Outputs:
- updated: float32 [256, 2048], P('slabs')
Inputs may be any that keep to these rules, and one draw needn't show every extreme that they name: `voxel_index`: within a row all 2048 positions are distinct and lie in a run of 4096 consecutive positions, whose first and last position are both in the row.
All inputs are finite; a program needn't handle non-finite values.
Results may differ from a plain program's by a relative error of at most 0.0003.
Values may be sent and summed in bfloat16 or wider, within the bound.
A program may use at most 64 MiB of HBM per device.

v0:
```python
import jax
import jax.numpy as jnp
from jax import lax
from jax.sharding import PartitionSpec as P

BLOCK_SIZE = 8
SWEEPS = 2


def padded(block, sides, width):
    for axis, dim in sides:
        count = lax.axis_size(axis)
        forward = [(i, i + 1) for i in range(count - 1)]
        backward = [(target, source) for source, target in forward]
        low = lax.ppermute(
            lax.slice_in_dim(block, block.shape[dim] - width, None, axis=dim), axis, forward
        )
        high = lax.ppermute(lax.slice_in_dim(block, 0, width, axis=dim), axis, backward)
        block = jnp.concatenate([low, block, high], axis=dim)
    return block


def shifted(value, axis, steps):
    count = lax.axis_size(axis)
    leading, last = (max(0, -steps), min(count, count - steps))
    return lax.ppermute(value, axis, [(source, source + steps) for source in range(leading, last)])


def transposed(left, right):
    return lax.dot_general(
        left, right, (((0,), (0,)), ((), ())), preferred_element_type=jnp.float32
    )


def product(left, right):
    return jnp.dot(left, right, precision=lax.Precision.HIGHEST, preferred_element_type=jnp.float32)


def pull_halves(g_rows, state, from_left, from_right):
    source_dev = state.shape[0]
    half = from_left.shape[1]
    g_left = g_rows[:, :source_dev]
    g_mid = g_rows[:, source_dev : 2 * source_dev]
    g_right = g_rows[:, 2 * source_dev :]
    first = product(g_left, from_left) + product(g_mid, state[:, :half])
    second = product(g_mid, state[:, half:]) + product(g_right, from_right)
    return jnp.concatenate([first, second], axis=1)


def sweep_blocks(current, left_rows, right_rows, stat, gram, support, block_order, puller):
    source_dev = current.shape[0]
    diagonal = jnp.diagonal(gram[:, source_dev : 2 * source_dev]) + 1.0

    def one_block(state, blk):
        start = blk * BLOCK_SIZE
        g_rows = lax.dynamic_slice_in_dim(gram, start, BLOCK_SIZE, 0)
        pulled = puller(g_rows, state, left_rows, right_rows)
        old = lax.dynamic_slice_in_dim(state, start, BLOCK_SIZE, 0)
        stat_rows = lax.dynamic_slice_in_dim(stat, start, BLOCK_SIZE, 0)
        mask_rows = lax.dynamic_slice_in_dim(support, start, BLOCK_SIZE, 0)
        scale = lax.dynamic_slice_in_dim(diagonal, start, BLOCK_SIZE, 0)
        fresh = mask_rows * jnp.maximum(old + (stat_rows - pulled) / scale[:, None], 0.0)
        return (lax.dynamic_update_slice_in_dim(state, fresh, start, 0), None)

    result, unused = lax.scan(one_block, current, block_order)
    return result


def local(movie, traces, voxel_index, footprint, block_order):
    voxel_dev = movie.shape[1]
    source_dev = traces.shape[1]
    extent = 2 * voxel_dev
    extended = padded(movie, (("slabs", 1),), voxel_dev // 2)
    nearby = padded(traces, (("slabs", 1),), source_dev)
    stat_part = transposed(traces, extended)
    gram_part = transposed(traces, nearby)
    rows = jnp.arange(source_dev)[:, None]
    dense = jnp.zeros((source_dev, extent), jnp.float32).at[rows, voxel_index].set(footprint)
    support = jnp.zeros((source_dev, extent), jnp.float32).at[rows, voxel_index].set(1.0)
    stat, gram = lax.psum((stat_part, gram_part), "frames")
    for sweep in range(SWEEPS):
        from_left = shifted(dense[:, voxel_dev:], "slabs", 1)
        from_right = shifted(dense[:, :voxel_dev], "slabs", -1)
        dense = sweep_blocks(
            dense, from_left, from_right, stat, gram, support, block_order, pull_halves
        )
    return dense[rows, voxel_index]


def solution(mesh):
    in_specs = (P("frames", "slabs"), P("frames", "slabs"), P("slabs", None), P("slabs", None), P())
    out_specs = P("slabs", None)
    return jax.shard_map(local, mesh=mesh, in_specs=in_specs, out_specs=out_specs, check_vma=False)
```

profile of v0, /device:TPU:1, one launch (start us, length us, event | category | flops | bytes accessed | tf_op | source)
XLA Modules:
  0.0 579.6 jit_solution(10739176513161037438)
XLA Ops:
  6.5 4.7 collective-permute-start.2
  11.2 1.9 collective-permute-start.3
  13.1 0.9 fusion.26
  14.1 0.0 copy-start.7
  14.1 0.1 multiply_reduce_fusion
  14.2 0.5 copy-done.7
  14.7 0.1 and_reduce_fusion
  14.8 0.0 copy-start.4
  14.9 0.8 copy-done.4
  15.8 120.1 %scatter_custom_fusion = f32[65536]{0:T(1024)S(1)} fusion(s32[32768]{0:T(1024)S(1)} %bitcast.41, f32[32768]{0:T(1024)S(1)} %bitcast.43, f32[]{:T(128)} %constant.34.clone.1), kind=kCustom, calls=%fused_computation.48 | custom fusion | bytes 262148
  135.9 0.1 reshape.11
  136.0 0.0 copy-start.3
  136.0 3.6 collective-permute-start.4
  139.7 1.9 collective-permute-start
  141.6 2.4 collective-permute-start.1
  144.0 120.1 %scatter_custom_fusion.1 = f32[65536]{0:T(1024)S(1)} fusion(s32[32768]{0:T(1024)S(1)} %bitcast.42, f32[32768]{0:T(1024)S(1)} %broadcast.78, f32[]{:T(128)} %constant.34.clone.1), kind=kCustom, calls=%fused_computation.46 | custom fusion | bytes 262148
  264.2 0.0 copy-start.5
  264.2 0.1 reshape.15
  264.2 1.9 collective-permute-start.5
  266.2 0.9 convolution_bitcast_fusion
  267.1 0.0 all-reduce.2.cloned.1.call-update
  267.2 0.2 convolution_bitcast_fusion.1
  267.4 3.8 psum.15
  271.2 0.1 slice.65
  271.3 0.7 gather_fusion
  271.9 20.1 %all-reduce.2.cloned.1.call-done = f32[16,4096]{1,0:T(8,128)} async-done(((f32[16,4096]{1,0:T(8,128)}), f32[16,4096]{1,0:T(8,128)}) %all-reduce.2.cloned.1.call-update) | async-done | bytes 262160 | tf_op jit(solution)/shard_map/psum | solution.py:80
  292.1 5.8 %while.20 = (s32[]{:T(128)}, f32[16,4096]{1,0:T(8,128)S(1)}, s32[2]{0:T(128)S(1)}, f32[16,4096]{1,0:T(8,128)S(1)}, f32[16,4096]{1,0:T(8,128)}, /*index=5*/f32[16...) while((s32[]{:T(128)}, f32[16,4096]{1,0:T(8,128)S(1)}, ...), condition=%wide.region_5.6_spmd, body=%wide.region_4.5_spmd.sunk | while | flops 12812294 | bytes 2636575 | solution.py:65
  292.1 0.7 dynamic_slice.61
  293.4 0.2 fusion.83
  293.7 0.3 convolution_add_fusion.9
  293.9 0.3 fusion.82
  294.2 0.3 convolution_add_fusion.8
  294.5 0.1 dynamic_slice.62
  294.5 0.3 copy-done
  294.9 0.1 fusion.84
  295.0 0.7 dynamic_slice.61
  296.4 0.2 fusion.83
  296.6 0.3 convolution_add_fusion.9
  296.9 0.3 fusion.82
  297.1 0.3 convolution_add_fusion.8
  297.4 0.1 dynamic_slice.62
  297.5 0.3 copy-done
  297.8 0.1 fusion.84
  297.9 0.0 copy-start.2
  297.9 4.2 collective-permute-start.6
  302.2 2.1 collective-permute-start.7
  304.4 4.3 collective-permute-done.7
  308.6 5.0 while.21
  308.6 0.6 dynamic_slice.67
  309.9 0.2 fusion.94
  310.1 0.3 convolution_add_fusion.11
  310.4 0.3 fusion.93
  310.7 0.3 convolution_add_fusion.10
  310.9 0.1 dynamic_slice.68
  311.0 0.1 fusion.95
  311.1 0.6 dynamic_slice.67
  312.4 0.2 fusion.94
  312.6 0.3 convolution_add_fusion.11
  312.9 0.3 fusion.93
  313.1 0.3 convolution_add_fusion.10
  313.4 0.1 dynamic_slice.68
  313.5 0.1 fusion.95
  313.6 258.4 %gather_fusion.1 = f32[32768]{0:T(1024)S(1)} fusion(f32[16,4096]{1,0:T(8,128)S(1)} %get-tuple-element.100, s32[32768]{0:T(1024)S(1)} %bitcast.39), kind=kCustom, calls=%fused_computation.1 | custom fusion | bytes 524288 | tf_op jit(solution)/shard_map/gather | solution.py:87
  572.0 0.7 reshape.25
  (35 shorter events, 0.3 us)
Async XLA Ops:
  6.5 7.6 %copy-start.6 = (s32[2]{0:T(128)S(1)}, s32[2]{0:T(128)}, u32[]{:S(2)}) copy-start(s32[2]{0:T(128)} %constant.46) | copy-start | bytes 28
  6.5 285.5 %all-reduce.2.cloned.1.call-start = ((), (), s32[]{:S(2)}) async-start(), calls=%async_computation | async-start | bytes 524288 | tf_op jit(solution)/shard_map/psum | solution.py:80
  6.5 260.6 %collective-permute-start.2 = (bf16[8,16]{1,0:T(8,128)(2,1)}, bf16[8,16]{1,0:T(8,128)(2,1)S(1)}, u32[]{:S(2)}, u32[]{:S(2)}) collective-permute-start(bf16[8,16]{1,0:T(8,128)(2,1)} %param.10), channel_id=1, source_target_pairs={{0,1},{1,2},{2,3},{3,4},{4,5},{5,6},{6,7},{7,8},{8,9},{9,10},{10,1... | collective-permute-start | bytes 776 | tf_op jit(solution)/shard_map/ppermute | solution.py:15
  11.2 256.0 %collective-permute-start.3 = (bf16[8,16]{1,0:T(8,128)(2,1)}, bf16[8,16]{1,0:T(8,128)(2,1)S(1)}, u32[]{:S(2)}, u32[]{:S(2)}) collective-permute-start(bf16[8,16]{1,0:T(8,128)(2,1)} %param.10), channel_id=1, source_target_pairs={{1,0},{2,1},{3,2},{4,3},{5,4},{6,5},{7,6},{8,7},{9,8},{10,9},{11,1... | collective-permute-start | bytes 776 | tf_op jit(solution)/shard_map/ppermute | solution.py:18
  14.1 0.7 copy-start.7
  14.8 0.9 copy-start.4
  136.0 3.7 copy-start.3
  136.0 135.9 %collective-permute-start.4 = (f32[16,2048]{1,0:T(8,128)S(1)}, f32[16,2048]{1,0:T(8,128)S(1)}, u32[]{:S(2)}, u32[]{:S(2)}) collective-permute-start(f32[16,2048]{1,0:T(8,128)S(1)} %get-tuple-element.140), channel_id=1, source_target_pairs={{0,1},{1,2},{2,3},{3,4},{4,5},{5,6},{6,7},{7,8},{8,9},{9,10},{10,1... | collective-permute-start | bytes 393224 | tf_op jit(solution)/shard_map/ppermute | solution.py:26
  139.7 124.6 %collective-permute-start = (bf16[8,1024]{1,0:T(8,128)(2,1)S(1)}, bf16[8,1024]{1,0:T(8,128)(2,1)S(1)}, u32[]{:S(2)}, u32[]{:S(2)}) collective-permute-start(bf16[8,1024]{1,0:T(8,128)(2,1)S(1)} %get-tuple-element.141), channel_id=1, source_target_pairs={{0,1},{1,2},{2,3},{3,4},{4,5},{5,6},{6,7},{7,8},{8,9},{9,10},{10,1... | collective-permute-start | bytes 49160 | tf_op jit(solution)/shard_map/ppermute | solution.py:15
  141.6 124.6 %collective-permute-start.1 = (bf16[8,1024]{1,0:T(8,128)(2,1)S(1)}, bf16[8,1024]{1,0:T(8,128)(2,1)S(1)}, u32[]{:S(2)}, u32[]{:S(2)}) collective-permute-start(bf16[8,1024]{1,0:T(8,128)(2,1)S(1)} %get-tuple-element.142), channel_id=1, source_target_pairs={{1,0},{2,1},{3,2},{4,3},{5,4},{6,5},{7,6},{8,7},{9,8},{10,9},{11,1... | collective-permute-start | bytes 49160 | tf_op jit(solution)/shard_map/ppermute | solution.py:18
  264.2 2.0 copy-start.5
  264.2 7.7 %collective-permute-start.5 = (f32[16,2048]{1,0:T(8,128)S(1)}, f32[16,2048]{1,0:T(8,128)S(1)}, u32[]{:S(2)}, u32[]{:S(2)}) collective-permute-start(f32[16,2048]{1,0:T(8,128)S(1)} %get-tuple-element.139), channel_id=1, source_target_pairs={{1,0},{2,1},{3,2},{4,3},{5,4},{6,5},{7,6},{8,7},{9,8},{10,9},{11,1... | collective-permute-start | bytes 393224 | tf_op jit(solution)/shard_map/ppermute | solution.py:26
  271.3 20.8 %copy-start.8 = (s32[2]{0:T(128)S(1)}, s32[2]{0:T(128)}, u32[]{:S(2)}) copy-start(s32[2]{0:T(128)} %param.13) | copy-start | bytes 28
  293.9 1.0 copy-start
  296.8 1.0 copy-start
  297.9 6.4 %copy-start.2 = (s32[16,2048]{1,0:T(8,128)S(1)}, s32[16,2048]{1,0:T(8,128)}, u32[]{:S(2)}) copy-start(s32[16,2048]{1,0:T(8,128)} %param.11) | copy-start | bytes 393220
  297.9 6.4 %collective-permute-start.6 = (f32[16,2048]{1,0:T(8,128)S(1)}, f32[16,2048]{1,0:T(8,128)S(1)}, u32[]{:S(2)}, u32[]{:S(2)}) collective-permute-start(f32[16,2048]{1,0:T(8,128)S(1)} %get-tuple-element.138), channel_id=1, source_target_pairs={{0,1},{1,2},{2,3},{3,4},{4,5},{5,6},{6,7},{7,8},{8,9},{9,10},{10,1... | collective-permute-start | bytes 393224 | tf_op jit(solution)/shard_map/ppermute | solution.py:26
  302.2 6.4 %copy-start.1 = (f32[16,4096]{1,0:T(8,128)S(1)}, f32[16,4096]{1,0:T(8,128)}, u32[]{:S(2)}) copy-start(f32[16,4096]{1,0:T(8,128)} %get-tuple-element.334) | copy-start | bytes 786436
  302.2 6.4 %collective-permute-start.7 = (f32[16,2048]{1,0:T(8,128)S(1)}, f32[16,2048]{1,0:T(8,128)S(1)}, u32[]{:S(2)}, u32[]{:S(2)}) collective-permute-start(f32[16,2048]{1,0:T(8,128)S(1)} %get-tuple-element.137), channel_id=1, source_target_pairs={{1,0},{2,1},{3,2},{4,3},{5,4},{6,5},{7,6},{8,7},{9,8},{10,9},{11,1... | collective-permute-start | bytes 393224 | tf_op jit(solution)/shard_map/ppermute | solution.py:26
Sparse Core Ops, SparseCore 0:
  267.3 24.7 all-reduce.1
where the time goes:
time: 580 us
  local copies, waits for them, and re-layouts  505 us (87%)
  waiting for transfers between devices  24.4 us (4%)
  starting transfers between devices  22.8 us (4%)
  between operations  13.7 us (2%)
    gather x2, local copies, waits for them, and re-layouts, local(): return dense[rows, voxel_index]  259 us
    unnamed x22, local copies, waits for them, and re-layouts  242 us
    psum x1, waiting for transfers between devices, local(): stat, gram = lax.psum((stat_part, gram_part), 'frames')  20.1 us
    ppermute x4, starting transfers between devices, shifted(): lax.ppermute(value, axis, [(source, source + steps) for source in range(l...  11.9 us
  transfers between devices with their start and end apart: 9, of which 2 were waited for; matrix products, arithmetic and copies ran while one was open for 42% of the time, Pallas kernels for 0%

commit v1 on v0

v1 whole, which is shorter than its diff:
```python
import functools

import jax
import jax.numpy as jnp
from jax import lax
from jax.experimental import pallas as pl
from jax.experimental.pallas import tpu as pltpu
from jax.sharding import PartitionSpec as P

BLOCK = 8
LANES = 128
MESH = pl.DeviceIdType.MESH
F32 = jnp.float32
BF16 = jnp.bfloat16


def dot_nt(left, right):
    return lax.dot_general(left, right, (((1,), (1,)), ((), ())), preferred_element_type=F32)


def dot_nn(left, right):
    return lax.dot_general(left, right, (((1,), (0,)), ((), ())), preferred_element_type=F32)


def halves(value):
    high = value.astype(BF16)
    low = (value - high.astype(F32)).astype(BF16)
    return high, low


def kernel(
    nf, ns, order_ref, movie_ref, traces_ref, index_ref, foot_ref, out_ref,
    own, left, right, dense, dense_l, dense_r, final, hi_s, lo_s, vh_s, vl_s,
    send_m, recv_m, send_d, recv_d,
):
    f = lax.axis_index("frames")
    s = lax.axis_index("slabs")
    has_l = s > 0
    has_r = s < ns - 1
    frames, voxels = movie_ref.shape
    margin = voxels // 2
    extent = 2 * voxels
    chunks = extent // LANES
    half = chunks // 2
    foot_n = foot_ref.shape[1]

    barrier = pltpu.get_barrier_semaphore()
    for d in range(1, nf):
        pl.semaphore_signal(barrier, inc=1, device_id=(lax.rem(f + d, nf), s), device_id_type=MESH)

    @pl.when(has_l)
    def _():
        for d in range(nf):
            pl.semaphore_signal(
                barrier, inc=1, device_id=(lax.rem(f + d, nf), s - 1), device_id_type=MESH)

    @pl.when(has_r)
    def _():
        for d in range(nf):
            pl.semaphore_signal(
                barrier, inc=1, device_id=(lax.rem(f + d, nf), s + 1), device_id_type=MESH)

    own[f, :, 0:margin] = movie_ref[:, 0:margin].astype(F32)
    own[f, :, margin + LANES:] = movie_ref[:, margin:].astype(F32)
    own[f, :, margin:margin + LANES] = jnp.zeros((frames, LANES), F32)
    own[f, :, margin:margin + 2 * BLOCK] = traces_ref[...].astype(F32)

    @pl.when(jnp.logical_not(has_l))
    def _():
        left[...] = jnp.zeros_like(left)
        dense_l[...] = jnp.full(dense_l.shape, -1.0, F32)

    @pl.when(jnp.logical_not(has_r))
    def _():
        right[...] = jnp.zeros_like(right)
        dense_r[...] = jnp.full(dense_r.shape, -1.0, F32)

    swap = order_ref[0] != 0

    def permuted(ref):
        a = ref[0:BLOCK, :]
        b = ref[BLOCK:2 * BLOCK, :]
        return jnp.concatenate([jnp.where(swap, b, a), jnp.where(swap, a, b)], axis=0)

    index = permuted(index_ref)
    value = permuted(foot_ref)
    hi_s[...] = (index >> 7).astype(F32)
    lo_s[...] = (index & (LANES - 1)).astype(F32)
    v_hi = value.astype(BF16).astype(F32)
    vl_s[...] = value - v_hi
    vh_s[...] = jnp.where(v_hi == 0.0, -1.0, v_hi)

    def peer(d):
        to = lax.rem(f + d, nf)
        return pltpu.make_async_remote_copy(
            src_ref=own.at[f], dst_ref=own.at[f], send_sem=send_m.at[0, to],
            recv_sem=recv_m.at[0, f], device_id=(to, s), device_id_type=MESH)

    def to_right(d):
        to = lax.rem(f + d, nf)
        return pltpu.make_async_remote_copy(
            src_ref=own.at[f, :, pl.ds(margin, margin + LANES)], dst_ref=left.at[f],
            send_sem=send_m.at[1, to], recv_sem=recv_m.at[1, f],
            device_id=(to, s + 1), device_id_type=MESH)

    def to_left(d):
        to = lax.rem(f + d, nf)
        return pltpu.make_async_remote_copy(
            src_ref=own.at[f, :, pl.ds(0, margin + LANES)], dst_ref=right.at[f],
            send_sem=send_m.at[2, to], recv_sem=recv_m.at[2, f],
            device_id=(to, s - 1), device_id_type=MESH)

    count = nf - 1 + nf * has_l.astype(jnp.int32) + nf * has_r.astype(jnp.int32)
    pl.semaphore_wait(barrier, count)

    for d in range(1, nf):
        peer(d).start()

    @pl.when(has_r)
    def _():
        for d in range(nf):
            to_right(d).start()

    @pl.when(has_l)
    def _():
        for d in range(nf):
            to_left(d).start()

    rows16 = 2 * BLOCK
    iota = lax.broadcasted_iota(jnp.int32, (rows16, foot_n), 0).astype(F32)
    span = half * BLOCK

    def dense_right(b):
        return pltpu.make_async_remote_copy(
            src_ref=dense.at[pl.ds((2 * b + 1) * span, span), :],
            dst_ref=dense_l.at[pl.ds(b * span, span), :],
            send_sem=send_d.at[0, b], recv_sem=recv_d.at[0, b],
            device_id=(f, s + 1), device_id_type=MESH)

    def dense_left(b):
        return pltpu.make_async_remote_copy(
            src_ref=dense.at[pl.ds(2 * b * span, span), :],
            dst_ref=dense_r.at[pl.ds(b * span, span), :],
            send_sem=send_d.at[1, b], recv_sem=recv_d.at[1, b],
            device_id=(f, s - 1), device_id_type=MESH)

    for b in range(2):
        def scatter_row(k, carry, b=b):
            row = pl.ds(b * BLOCK + k, 1)

            def spread(ref):
                return jnp.broadcast_to(ref[row, :], (rows16, foot_n)).astype(BF16)

            hi = spread(hi_s)
            lo = spread(lo_s)
            vh = spread(vh_s)
            vl = spread(vl_s)
            zero = jnp.zeros((rows16, foot_n), BF16)
            one = jnp.ones((rows16, foot_n), BF16)
            iota16 = iota.astype(BF16)
            low = [jnp.where(lo == iota16 + BF16(16 * t), one, zero) for t in range(LANES // 16)]
            high = [hi == iota16 + BF16(16 * t) for t in range(chunks // 16)]
            lhs = [jnp.where(m, vh, zero) for m in high] + [jnp.where(m, vl, zero) for m in high]
            got = dot_nt(jnp.concatenate(lhs, axis=0), jnp.concatenate(low, axis=0))
            g_hi = got[:chunks]
            enc = jnp.where(g_hi == 0.0, -1.0, jnp.maximum(g_hi, 0.0) + got[chunks:])
            dense[pl.ds(b * chunks * BLOCK + k, chunks, stride=BLOCK), :] = enc
            return carry

        lax.fori_loop(0, BLOCK, scatter_row, 0)

        @pl.when(has_r)
        def _(b=b):
            dense_right(b).start()

        @pl.when(has_l)
        def _(b=b):
            dense_left(b).start()

    for d in range(1, nf):
        pltpu.make_async_remote_copy(
            src_ref=own.at[f], dst_ref=own.at[lax.rem(f + d, nf)], send_sem=send_m.at[0, 0],
            recv_sem=recv_m.at[0, lax.rem(f + d, nf)], device_id=(f, s),
            device_id_type=MESH).wait_recv()

    @pl.when(has_l)
    def _():
        for d in range(nf):
            pltpu.make_async_remote_copy(
                src_ref=left.at[d], dst_ref=left.at[d], send_sem=send_m.at[1, 0],
                recv_sem=recv_m.at[1, d], device_id=(f, s), device_id_type=MESH).wait_recv()

    @pl.when(has_r)
    def _():
        for d in range(nf):
            pltpu.make_async_remote_copy(
                src_ref=right.at[d], dst_ref=right.at[d], send_sem=send_m.at[2, 0],
                recv_sem=recv_m.at[2, d], device_id=(f, s), device_id_type=MESH).wait_recv()

    def all_frames(pick):
        return jnp.concatenate([pick(g) for g in range(nf)], axis=0)

    movie_l = jnp.concatenate([
        all_frames(lambda g: left[g, :, LANES:]),
        all_frames(lambda g: own[g, :, 0:margin])], axis=1).astype(BF16)
    movie_r = jnp.concatenate([
        all_frames(lambda g: own[g, :, margin + LANES:]),
        all_frames(lambda g: right[g, :, 0:margin])], axis=1).astype(BF16)
    total = nf * frames
    padding = jnp.zeros((LANES - total, LANES), F32)
    eye = (lax.broadcasted_iota(jnp.int32, (rows16, LANES), 0)
           == lax.broadcasted_iota(jnp.int32, (rows16, LANES), 1)).astype(F32).astype(BF16)

    def by_source(pick):
        block = jnp.concatenate([all_frames(pick), padding], axis=0).astype(BF16)
        rows = dot_nt(eye, block)
        return jnp.concatenate([jnp.where(swap, rows[BLOCK:], rows[:BLOCK]),
                                jnp.where(swap, rows[:BLOCK], rows[BLOCK:])], axis=0)

    t_own = by_source(lambda g: own[g, :, margin:margin + LANES])
    t_left = by_source(lambda g: left[g, :, 0:LANES])
    t_right = by_source(lambda g: right[g, :, margin:])

    depth = -(-(total + 3 * 32) // LANES) * LANES
    identity = (lax.broadcasted_iota(jnp.int32, (total, LANES), 0)
                == lax.broadcasted_iota(jnp.int32, (total, LANES), 1)).astype(F32)

    def weights(t_near):
        t32 = jnp.concatenate([t_own, t_near], axis=0)
        stacked = jnp.concatenate(
            [identity, t32, t32, t32,
             jnp.zeros((depth - total - 96, LANES), F32)], axis=0).astype(BF16)
        full = dot_nt(t32.astype(BF16), stacked)
        lane = lax.broadcasted_iota(jnp.int32, full.shape, 1)
        g_hi = full.astype(BF16).astype(F32)
        picked = jnp.where((lane >= total + 32) & (lane < total + 64), full - g_hi, g_hi)
        first = jnp.where(lane < total, full, -picked).astype(BF16)
        t_f = jnp.concatenate([t32[0:8], t32[16:24]], axis=0)
        t_s = jnp.concatenate([t32[8:16], t32[24:32]], axis=0)
        stacked2 = jnp.concatenate(
            [t_f, t_f, t_f, jnp.zeros((LANES - 48, LANES), F32)], axis=0).astype(BF16)
        cross = dot_nt(t_s.astype(BF16), stacked2)
        lane2 = lax.broadcasted_iota(jnp.int32, cross.shape, 1)
        row2 = lax.broadcasted_iota(jnp.int32, cross.shape, 0)
        c_hi = cross.astype(BF16).astype(F32)
        picked2 = jnp.where((lane2 >= 16) & (lane2 < 32), cross - c_hi, c_hi)
        same = (row2 // 8) == ((lane2 // 8) % 2)
        second = jnp.where(same, picked2, 0.0).astype(BF16)
        inverse = 1.0 / (jnp.sum(t32 * t32, axis=1, keepdims=True) + 1.0)
        return first, second, inverse

    w_l, c_l, inv_l = weights(t_left)
    w_r, c_r, inv_r = weights(t_right)

    @pl.when(has_l)
    def _():
        for b in range(2):
            pltpu.make_async_remote_copy(
                src_ref=dense_l.at[pl.ds(b * span, span), :],
                dst_ref=dense_l.at[pl.ds(b * span, span), :],
                send_sem=send_d.at[0, 0], recv_sem=recv_d.at[0, b],
                device_id=(f, s), device_id_type=MESH).wait_recv()

    @pl.when(has_r)
    def _():
        for b in range(2):
            pltpu.make_async_remote_copy(
                src_ref=dense_r.at[pl.ds(b * span, span), :],
                dst_ref=dense_r.at[pl.ds(b * span, span), :],
                send_sem=send_d.at[1, 0], recv_sem=recv_d.at[1, b],
                device_id=(f, s), device_id_type=MESH).wait_recv()

    def wide(ref, start):
        return jnp.concatenate(
            [ref[(start + c) * BLOCK:(start + c + 1) * BLOCK, :] for c in range(half)], axis=1)

    for side, (movie, w, cross, inverse, near) in enumerate(
            ((movie_l, w_l, c_l, inv_l, dense_l), (movie_r, w_r, c_r, inv_r, dense_r))):
        enc = [wide(dense, side * half), wide(dense, chunks + side * half),
               wide(near, 0), wide(near, half)]
        mask = [(e >= 0.0).astype(F32) for e in enc]
        state = [jnp.maximum(e, 0.0) for e in enc]
        pad = jnp.zeros((depth - total - 96, movie.shape[1]), BF16)
        pad2 = jnp.zeros((LANES - 48, movie.shape[1]), BF16)

        def residual(w_rows, state):
            high, low = halves(jnp.concatenate(state, axis=0))
            return dot_nn(w_rows, jnp.concatenate([movie, high, high, low, pad], axis=0))

        def change(c_rows, old, new):
            high, low = halves(jnp.concatenate([n - o for n, o in zip(new, old)], axis=0))
            return dot_nn(c_rows, jnp.concatenate([high, high, low, pad2], axis=0))

        def step(i, rest):
            return mask[i] * jnp.maximum(state[i] + rest * inverse[8 * i:8 * i + 8], 0.0)

        rest = residual(w, state)
        new_f = [step(0, rest[0:8]), step(2, rest[16:24])]
        moved = change(cross, [state[0], state[2]], new_f)
        new_s = [step(1, rest[8:16] - moved[0:8]), step(3, rest[24:32] - moved[8:16])]
        state = [new_f[0], new_s[0], new_f[1], new_s[1]]
        rest = residual(w[0:16], state)
        new_f = step(0, rest[0:8])
        moved = change(cross, [state[0], state[2]], [new_f, state[2]])
        new_s = step(1, rest[8:16] - moved[0:8])
        for c in range(half):
            at = (side * half + c) * BLOCK
            cut = slice(c * LANES, (c + 1) * LANES)
            final[at:at + BLOCK, :] = jnp.where(swap, new_s[:, cut], new_f[:, cut])
            at = at + chunks * BLOCK
            final[at:at + BLOCK, :] = jnp.where(swap, new_f[:, cut], new_s[:, cut])

    for b in range(2):
        place = index_ref[b * BLOCK:(b + 1) * BLOCK, :]
        tiles = foot_n // LANES
        chunk_of = [place[:, j * LANES:(j + 1) * LANES] >> 7 for j in range(tiles)]
        lane_of = [place[:, j * LANES:(j + 1) * LANES] & (LANES - 1) for j in range(tiles)]

        def pick(c, taken, b=b, chunk_of=chunk_of, lane_of=lane_of):
            at = pl.multiple_of((b * chunks + c) * BLOCK, BLOCK)
            tile = final[pl.ds(at, BLOCK), :]
            return tuple(
                jnp.where(chunk_of[j] == c,
                          jnp.take_along_axis(tile, lane_of[j], axis=1, mode="promise_in_bounds"),
                          taken[j])
                for j in range(tiles))

        taken = lax.fori_loop(
            0, chunks, pick, tuple(jnp.zeros((BLOCK, LANES), F32) for _ in range(tiles)))
        for j in range(tiles):
            out_ref[b * BLOCK:(b + 1) * BLOCK, j * LANES:(j + 1) * LANES] = taken[j]

    for d in range(1, nf):
        peer(d).wait_send()

    @pl.when(has_r)
    def _():
        for d in range(nf):
            to_right(d).wait_send()
        for b in range(2):
            dense_right(b).wait_send()

    @pl.when(has_l)
    def _():
        for d in range(nf):
            to_left(d).wait_send()
        for b in range(2):
            dense_left(b).wait_send()


def local(movie, traces, voxel_index, footprint, block_order):
    nf = lax.axis_size("frames")
    ns = lax.axis_size("slabs")
    frames, voxels = movie.shape
    sources, foot_n = footprint.shape
    margin = voxels // 2
    chunks = 2 * voxels // LANES
    vmem = pl.BlockSpec(memory_space=pltpu.VMEM)
    return pl.pallas_call(
        functools.partial(kernel, nf, ns),
        out_shape=jax.ShapeDtypeStruct((sources, foot_n), F32),
        in_specs=[pl.BlockSpec(memory_space=pltpu.SMEM)] + [vmem] * 4,
        out_specs=vmem,
        scratch_shapes=[
            pltpu.VMEM((nf, frames, voxels + LANES), F32),
            pltpu.VMEM((nf, frames, margin + LANES), F32),
            pltpu.VMEM((nf, frames, margin + LANES), F32),
            pltpu.VMEM((sources * chunks, LANES), F32),
            pltpu.VMEM((sources * chunks // 2, LANES), F32),
            pltpu.VMEM((sources * chunks // 2, LANES), F32),
            pltpu.VMEM((sources * chunks, LANES), F32),
            pltpu.VMEM((sources, foot_n), F32),
            pltpu.VMEM((sources, foot_n), F32),
            pltpu.VMEM((sources, foot_n), F32),
            pltpu.VMEM((sources, foot_n), F32),
            pltpu.SemaphoreType.DMA((3, nf)),
            pltpu.SemaphoreType.DMA((3, nf)),
            pltpu.SemaphoreType.DMA((2, 2)),
            pltpu.SemaphoreType.DMA((2, 2)),
        ],
        compiler_params=pltpu.CompilerParams(
            collective_id=0, has_side_effects=True, vmem_limit_bytes=32 * 1024 * 1024),
        cost_estimate=pl.CostEstimate(
            flops=2 * sources * 64 * LANES * foot_n, bytes_accessed=500000, transcendentals=0),
    )(block_order, movie, traces, voxel_index, footprint)


def solution(mesh):
    in_specs = (P("frames", "slabs"), P("frames", "slabs"), P("slabs", None), P("slabs", None), P())
    out_specs = P("slabs", None)
    return jax.shard_map(local, mesh=mesh, in_specs=in_specs, out_specs=out_specs, check_vma=False)
```

time: 580 us -> 24.7 us (0.04)
  local copies, waits for them, and re-layouts: 505 us -> 4.56 us
  waiting for transfers between devices: 24.4 us -> 0 us
  starting transfers between devices: 22.8 us -> 0 us
  Pallas kernels: 0 us -> 19.9 us
  between operations: 13.7 us -> 0.01 us
    gather x3 -> x0, local copies, waits for them, and re-layouts: 260 us -> none  [the longest x2 259 us: local(): return dense[rows, voxel_index]]
    unnamed x22 -> x11, local copies, waits for them, and re-layouts: 242 us -> 4.56 us
    ppermute x8 -> x0, starting transfers between devices: 22.8 us -> none  [the longest x4 11.9 us: shifted(): lax.ppermute(value, axis, [(source, source + steps) for source in range(l...]
    psum x1 -> x0, waiting for transfers between devices: 20.1 us -> none  [local(): stat, gram = lax.psum((stat_part, gram_part), 'frames')]
    pallas_call x0 -> x1, Pallas kernels: none -> 19.9 us  [local(): pl.pallas_call(functools.partial(kernel, nf, ns), out_shape=jax.ShapeDtyp...]
  transfers between devices with their start and end apart: 9 -> 0, of which waited for: 2 -> 0; matrix products, arithmetic and copies ran while one was open for 42% -> 0% of each run, Pallas kernels for 0% -> 0%
where the time goes in v1:
time: 24.7 us; the launch traced here: 24.5 us
  Pallas kernels  19.9 us (81%)
  local copies, waits for them, and re-layouts  4.56 us (18%)
    pallas_call x1, Pallas kernels, local(): pl.pallas_call(functools.partial(kernel, nf, ns), out_shape=jax.ShapeDtyp...  19.9 us
    unnamed x11, local copies, waits for them, and re-layouts  4.56 us

profile of v1, /device:TPU:1, one launch (start us, length us, event | category | flops | bytes accessed | tf_op | source)
XLA Modules:
  0.0 24.5 jit_solution(10688362945582049632)
XLA Ops:
  0.0 0.0 copy-start
  0.0 0.9 %copy-done = s32[16,2048]{1,0:T(8,128)S(1)} copy-done((s32[16,2048]{1,0:T(8,128)S(1)}, s32[16,2048]{1,0:T(8,128)}, u32[]{:S(2)}) %copy-start) | copy-done | bytes 131096
  0.9 0.0 copy-start.1
  0.9 0.9 %copy-done.1 = f32[16,2048]{1,0:T(8,128)S(1)} copy-done((f32[16,2048]{1,0:T(8,128)S(1)}, f32[16,2048]{1,0:T(8,128)}, u32[]{:S(2)}) %copy-start.1) | copy-done | bytes 131096
  1.8 0.0 copy-start.2
  1.8 0.8 %copy-done.2 = bf16[8,2048]{1,0:T(8,128)(2,1)S(1)} copy-done((bf16[8,2048]{1,0:T(8,128)(2,1)S(1)}, bf16[8,2048]{1,0:T(8,128)(2,1)}, u32[]{:S(2)}) %copy-start.2) | copy-done | bytes 32792
  2.6 0.0 copy-start.3
  2.6 0.7 %copy-done.3 = bf16[8,16]{1,0:T(8,128)(2,1)S(1)} copy-done((bf16[8,16]{1,0:T(8,128)(2,1)S(1)}, bf16[8,16]{1,0:T(8,128)(2,1)}, u32[]{:S(2)}) %copy-start.3) | copy-done | bytes 280
  3.3 0.0 copy-start.4
  3.3 0.7 %copy-done.4 = s32[2]{0:T(128)S(1)} copy-done((s32[2]{0:T(128)S(1)}, s32[2]{0:T(128)}, u32[]{:S(2)}) %copy-start.4) | copy-done | bytes 32
  3.9 19.9 %shard_map.55 = f32[16,2048]{1,0:T(8,128)S(1)} custom-call(s32[2]{0:T(128)S(1)} %copy-done.4, bf16[8,2048]{1,0:T(8,128)(2,1)S(1)} %copy-done.2, bf16[8,16]{1,0:T(8,128)(2,1)S(1)} %copy-done.3, s32[16,2048]{1,0:T(8,128)S(1)} %copy-done, f32[16,2048]{1,0:T(8,128)S(1)} %copy-done.1), custom_call_target="tpu_custom_call" | custom-call | flops 536870912 | bytes 500000 | tf_op jit(solution)/shard_map/pallas_call | solution.py:359
  23.8 0.7 %copy.7 = f32[16,2048]{1,0:T(8,128)} copy(f32[16,2048]{1,0:T(8,128)S(1)} %shard_map.55) | data formatting | bytes 262144
Async XLA Ops:
  0.0 0.9 %copy-start = (s32[16,2048]{1,0:T(8,128)S(1)}, s32[16,2048]{1,0:T(8,128)}, u32[]{:S(2)}) copy-start(s32[16,2048]{1,0:T(8,128)} %index_ref.1) | copy-start | bytes 393220
  0.9 0.9 %copy-start.1 = (f32[16,2048]{1,0:T(8,128)S(1)}, f32[16,2048]{1,0:T(8,128)}, u32[]{:S(2)}) copy-start(f32[16,2048]{1,0:T(8,128)} %foot_ref.1) | copy-start | bytes 393220
  1.8 0.8 %copy-start.2 = (bf16[8,2048]{1,0:T(8,128)(2,1)S(1)}, bf16[8,2048]{1,0:T(8,128)(2,1)}, u32[]{:S(2)}) copy-start(bf16[8,2048]{1,0:T(8,128)(2,1)} %movie_ref.1) | copy-start | bytes 98308
  2.6 0.7 %copy-start.3 = (bf16[8,16]{1,0:T(8,128)(2,1)S(1)}, bf16[8,16]{1,0:T(8,128)(2,1)}, u32[]{:S(2)}) copy-start(bf16[8,16]{1,0:T(8,128)(2,1)} %traces_ref.1) | copy-start | bytes 772
  3.3 0.7 %copy-start.4 = (s32[2]{0:T(128)S(1)}, s32[2]{0:T(128)}, u32[]{:S(2)}) copy-start(s32[2]{0:T(128)} %order_ref.1) | copy-start | bytes 28

commit v2 on v1

--- a/solution.py
+++ b/solution.py
@@ -29,9 +29,9 @@
 
 
 def kernel(
-    nf, ns, order_ref, movie_ref, traces_ref, index_ref, foot_ref, out_ref,
-    own, left, right, dense, dense_l, dense_r, final, hi_s, lo_s, vh_s, vl_s,
-    send_m, recv_m, send_d, recv_d,
+    nf, ns, order_in, movie_in, traces_in, index_in, foot_in, out_ref,
+    order_ref, movie_ref, traces_ref, index_ref, foot_ref, own, left, right, dense, dense_l, dense_r, final, hi_s, lo_s, vh_s, vl_s,
+    load_sem, send_m, recv_m, send_d, recv_d,
 ):
     f = lax.axis_index("frames")
     s = lax.axis_index("slabs")
@@ -60,6 +60,14 @@
             pl.semaphore_signal(
                 barrier, inc=1, device_id=(lax.rem(f + d, nf), s + 1), device_id_type=MESH)
 
+    pairs = ((index_in, index_ref), (foot_in, foot_ref), (order_in, order_ref),
+             (movie_in, movie_ref), (traces_in, traces_ref))
+    loads = [pltpu.make_async_copy(a, b, load_sem.at[i]) for i, (a, b) in enumerate(pairs)]
+    for load in loads:
+        load.start()
+
+    loads[3].wait()
+    loads[4].wait()
     own[f, :, 0:margin] = movie_ref[:, 0:margin].astype(F32)
     own[f, :, margin + LANES:] = movie_ref[:, margin:].astype(F32)
     own[f, :, margin:margin + LANES] = jnp.zeros((frames, LANES), F32)
@@ -75,6 +83,8 @@
         right[...] = jnp.zeros_like(right)
         dense_r[...] = jnp.full(dense_r.shape, -1.0, F32)
 
+    for load in loads[:3]:
+        load.wait()
     swap = order_ref[0] != 0
 
     def permuted(ref):
@@ -145,7 +155,7 @@
             device_id=(f, s - 1), device_id_type=MESH)
 
     for b in range(2):
-        def scatter_row(k, carry, b=b):
+        def scatter_row(k, b=b):
             row = pl.ds(b * BLOCK + k, 1)
 
             def spread(ref):
@@ -165,9 +175,9 @@
             g_hi = got[:chunks]
             enc = jnp.where(g_hi == 0.0, -1.0, jnp.maximum(g_hi, 0.0) + got[chunks:])
             dense[pl.ds(b * chunks * BLOCK + k, chunks, stride=BLOCK), :] = enc
-            return carry
-
-        lax.fori_loop(0, BLOCK, scatter_row, 0)
+
+        for k in range(BLOCK):
+            scatter_row(k)
 
         @pl.when(has_r)
         def _(b=b):
@@ -316,17 +326,13 @@
         chunk_of = [place[:, j * LANES:(j + 1) * LANES] >> 7 for j in range(tiles)]
         lane_of = [place[:, j * LANES:(j + 1) * LANES] & (LANES - 1) for j in range(tiles)]
 
-        def pick(c, taken, b=b, chunk_of=chunk_of, lane_of=lane_of):
-            at = pl.multiple_of((b * chunks + c) * BLOCK, BLOCK)
-            tile = final[pl.ds(at, BLOCK), :]
-            return tuple(
-                jnp.where(chunk_of[j] == c,
-                          jnp.take_along_axis(tile, lane_of[j], axis=1, mode="promise_in_bounds"),
-                          taken[j])
-                for j in range(tiles))
-
-        taken = lax.fori_loop(
-            0, chunks, pick, tuple(jnp.zeros((BLOCK, LANES), F32) for _ in range(tiles)))
+        taken = [jnp.zeros((BLOCK, LANES), F32) for _ in range(tiles)]
+        for c in range(chunks):
+            at = (b * chunks + c) * BLOCK
+            tile = final[at:at + BLOCK, :]
+            for j in range(tiles):
+                got = jnp.take_along_axis(tile, lane_of[j], axis=1, mode="promise_in_bounds")
+                taken[j] = jnp.where(chunk_of[j] == c, got, taken[j])
         for j in range(tiles):
             out_ref[b * BLOCK:(b + 1) * BLOCK, j * LANES:(j + 1) * LANES] = taken[j]
 
@@ -359,9 +365,14 @@
     return pl.pallas_call(
         functools.partial(kernel, nf, ns),
         out_shape=jax.ShapeDtypeStruct((sources, foot_n), F32),
-        in_specs=[pl.BlockSpec(memory_space=pltpu.SMEM)] + [vmem] * 4,
+        in_specs=[pl.BlockSpec(memory_space=pltpu.HBM)] * 5,
         out_specs=vmem,
         scratch_shapes=[
+            pltpu.SMEM(block_order.shape, block_order.dtype),
+            pltpu.VMEM(movie.shape, movie.dtype),
+            pltpu.VMEM(traces.shape, traces.dtype),
+            pltpu.VMEM(voxel_index.shape, voxel_index.dtype),
+            pltpu.VMEM(footprint.shape, footprint.dtype),
             pltpu.VMEM((nf, frames, voxels + LANES), F32),
             pltpu.VMEM((nf, frames, margin + LANES), F32),
             pltpu.VMEM((nf, frames, margin + LANES), F32),
@@ -373,13 +384,14 @@
             pltpu.VMEM((sources, foot_n), F32),
             pltpu.VMEM((sources, foot_n), F32),
             pltpu.VMEM((sources, foot_n), F32),
+            pltpu.SemaphoreType.DMA((5,)),
             pltpu.SemaphoreType.DMA((3, nf)),
             pltpu.SemaphoreType.DMA((3, nf)),
             pltpu.SemaphoreType.DMA((2, 2)),
             pltpu.SemaphoreType.DMA((2, 2)),
         ],
         compiler_params=pltpu.CompilerParams(
-            collective_id=0, has_side_effects=True, vmem_limit_bytes=32 * 1024 * 1024),
+            collective_id=0, has_side_effects=True, vmem_limit_bytes=60 * 1024 * 1024),
         cost_estimate=pl.CostEstimate(
             flops=2 * sources * 64 * LANES * foot_n, bytes_accessed=500000, transcendentals=0),
     )(block_order, movie, traces, voxel_index, footprint)

time: 24.7 us -> 15.5 us (0.63)
  the two profiles are of different devices: /device:TPU:1 before, /device:TPU:9 now
where the time goes in v2:
time: 15.5 us; the launch traced here: 15.3 us
  Pallas kernels  13.8 us (89%)
  local copies, waits for them, and re-layouts  1.57 us (10%)
    pallas_call x1, Pallas kernels, local(): pl.pallas_call(functools.partial(kernel, nf, ns), out_shape=jax.ShapeDtyp...  13.8 us
    unnamed x1, local copies, waits for them, and re-layouts  1.57 us

profile of v2, /device:TPU:9, one launch (start us, length us, event | category | flops | bytes accessed | tf_op | source)
XLA Modules:
  0.0 15.3 jit_solution(15318786129815491260)
XLA Ops:
  0.0 13.8 %shard_map.55 = f32[16,2048]{1,0:T(8,128)} custom-call(s32[2]{0:T(128)} %order_in.1, bf16[8,2048]{1,0:T(8,128)(2,1)} %movie_in.1, bf16[8,16]{1,0:T(8,128)(2,1)} %traces_in.1, s32[16,2048]{1,0:T(8,128)} %index_in.1, f32[16,2048]{1,0:T(8,128)} %foot_in.1), custom_call_target="tpu_custom_call" | custom-call | flops 536870912 | bytes 500000 | tf_op jit(solution)/shard_map/pallas_call | solution.py:365
  13.8 1.6 %copy.7 = f32[16,2048]{1,0:T(8,128)} copy(f32[16,2048]{1,0:T(8,128)} %shard_map.55) | data formatting | bytes 262144
